TPU v7x, 256 devices: a whole 4x4x8 slice. The times are simulated.
256 devices in a mesh: src: 16 (over z, x_hi), tgt: 16 (over x_lo, y, core).
Axes of the slice: x: 4 (x_hi: 2, x_lo: 2; x = x_hi * 2 + x_lo), y: 4, z: 8, core: 2. Of those that a mesh axis runs over, the one named last changes fastest.
Arguments:
- src_emb: bfloat16 [64, 32768], P(None, 'src'), may hold values from -2.75 to 2.75
- tgt_emb: bfloat16 [64, 131072], P(None, 'tgt'), may hold values from -2.75 to 2.75
- target_features: bfloat16 [128, 131072], P(None, 'tgt'), may hold values from -6 to 6
- src_mass: float32 [32768], P('src'), may hold values from 1 to 10
- tgt_mass: float32 [131072], P('tgt'), may hold values from 1 to 10
- kept_blocks: int32 [128, 128], P('src', 'tgt'), may hold values from 0 to 31, as said below
- kept_count: int32 [128, 16], P('src', 'tgt'), may hold values from 1 to 8
Outputs:
- projected: float32 [32768, 128], P(('src', 'tgt'))
- src_potential: float32 [32768], P('src')
- tgt_potential: float32 [131072], P('tgt')
Inputs may be any that keep to these rules, and one draw needn't show every extreme that they name: `kept_blocks`: entry [r, t * 8 + k] is a block number within target shard t; the 8 entries of one group are distinct; the first kept_count[r, t] of them are kept, the others are unused; every target block is kept by some source block row.
All inputs are finite; a program needn't handle non-finite values.
Results may differ from a plain program's by a relative error of at most 0.00075.
Values sent between devices are 32-bit elements; how exact they have to be, the bound alone decides.
A program may use at most 64 MiB of HBM per device.

v0:
```python
import jax
import jax.numpy as jnp
from jax import lax
from jax.sharding import PartitionSpec as P

BLOCK = 256
ITERS = 2


SENTINEL = -1e30
EPSILON = 0.1


def pair_distance(src_tile, norm_tile, tgt_chosen, tgt_norm_chosen):
    products = jnp.einsum("dr,dkc->krc", src_tile, tgt_chosen, preferred_element_type=jnp.float32)
    return norm_tile[None, :, None] + tgt_norm_chosen[:, None, :] - 2.0 * products


def merge_rows(highest, totals):
    overall = lax.pmax(highest, "tgt")
    return (overall, lax.psum(totals * jnp.exp(highest - overall), "tgt"))


def merge_columns(block_top, block_sum):
    overall = lax.pmax(block_top, "src")
    return (overall, lax.psum(block_sum * jnp.exp(block_top - overall), "src"))


def shards(src_emb, tgt_emb, target_features, src_mass, tgt_mass, kept_blocks, kept_count):
    emb_width = src_emb.shape[0]
    src_rows = src_emb.shape[1]
    tgt_rows = tgt_emb.shape[1]
    src_blocks = src_rows // BLOCK
    tgt_blocks = tgt_rows // BLOCK
    slot_count = kept_blocks.shape[1]
    src_tiles = src_emb.reshape(emb_width, src_blocks, BLOCK).transpose(1, 0, 2)
    src_norm = jnp.sum(jnp.square(src_emb.astype(jnp.float32)), axis=0).reshape(src_blocks, BLOCK)
    tgt_tiles = tgt_emb.reshape(emb_width, tgt_blocks, BLOCK)
    target_norm = jnp.sum(jnp.square(tgt_emb.astype(jnp.float32)), axis=0).reshape(
        tgt_blocks, BLOCK
    )
    feat_tiles = target_features.reshape(target_features.shape[0], tgt_blocks, BLOCK)
    live_slot = lax.broadcasted_iota(jnp.int32, (src_blocks, slot_count), 1) < kept_count
    packets = (src_tiles, src_norm, kept_blocks, live_slot)
    flat_index = kept_blocks.reshape(-1)
    member = (
        lax.broadcasted_iota(jnp.int32, (tgt_blocks, flat_index.shape[0]), 0) == flat_index[None, :]
    )

    def distances(packet):
        return pair_distance(
            packet[0],
            packet[1],
            jnp.take(tgt_tiles, packet[2], axis=1),
            jnp.take(target_norm, packet[2], axis=0),
        )

    def row_scaled(potential_tiles, packet):
        scaled = (
            jnp.take(potential_tiles, packet[2], axis=0)[:, None, :] - distances(packet)
        ) / EPSILON
        return jnp.where(packet[3][:, None, None], scaled, SENTINEL)

    tgt_potential = jnp.zeros((tgt_rows,), jnp.float32)
    src_potential = jnp.zeros((src_rows,), jnp.float32)
    for iteration in range(ITERS):
        row_potential_tiles = tgt_potential.reshape(tgt_blocks, BLOCK)

        def row_per_block(packet):
            scaled = row_scaled(row_potential_tiles, packet)
            highest = jnp.max(scaled, axis=(0, 2))
            totals = jnp.sum(
                jnp.where(packet[3][:, None, None], jnp.exp(scaled - highest[None, :, None]), 0.0),
                axis=(0, 2),
            )
            return (highest, totals)

        highest, totals = lax.map(row_per_block, packets)
        highest, totals = merge_rows(*(highest.reshape(src_rows), totals.reshape(src_rows)))
        src_potential = EPSILON * jnp.log(src_mass) - EPSILON * (highest + jnp.log(totals))
        column_potential_tiles = src_potential.reshape(src_blocks, BLOCK)

        def column_per_block(packet):
            scaled = (packet[4][None, :, None] - distances(packet)) / EPSILON
            scaled = jnp.where(packet[3][:, None, None], scaled, SENTINEL)
            highest = jnp.max(scaled, axis=1)
            totals = jnp.sum(
                jnp.where(packet[3][:, None, None], jnp.exp(scaled - highest[:, None, :]), 0.0),
                axis=1,
            )
            return (highest, totals)

        slot_top, slot_sum = lax.map(column_per_block, packets + (column_potential_tiles,))
        slot_top = slot_top.reshape(src_blocks * slot_count, BLOCK)
        slot_sum = slot_sum.reshape(src_blocks * slot_count, BLOCK)
        block_top = jnp.max(jnp.where(member[:, :, None], slot_top[None, :, :], SENTINEL), axis=1)
        scaled_sum = slot_sum * jnp.exp(slot_top - jnp.take(block_top, flat_index, axis=0))
        block_sum = jnp.dot(member.astype(jnp.float32), scaled_sum, precision=lax.Precision.HIGHEST)
        block_top, block_sum = merge_columns(
            *(block_top.reshape(tgt_rows), block_sum.reshape(tgt_rows))
        )
        tgt_potential = EPSILON * jnp.log(tgt_mass) - EPSILON * (block_top + jnp.log(block_sum))
    final_tiles = tgt_potential.reshape(tgt_blocks, BLOCK)

    def local_peak(packet):
        return jnp.max(row_scaled(final_tiles, packet), axis=(0, 2))

    local_top = lax.map(local_peak, packets)

    def weigh(packet):
        scaled = row_scaled(final_tiles, packet)
        weights = jnp.where(
            packet[3][:, None, None], jnp.exp(scaled - packet[4][None, :, None]), 0.0
        )
        rounded_count = lax.optimization_barrier(weights.astype(jnp.bfloat16))
        numerator = jnp.einsum(
            "krc,fkc->rf",
            rounded_count,
            jnp.take(feat_tiles, packet[2], axis=1),
            preferred_element_type=jnp.float32,
        )
        return (numerator, jnp.sum(rounded_count.astype(jnp.float32), axis=(0, 2)))

    numerator, denominator = lax.map(weigh, packets + (local_top,))
    numerator = numerator.reshape(src_rows, target_features.shape[0])
    denominator = denominator.reshape(src_rows)
    local_top = local_top.reshape(src_rows)
    share_rows = src_rows // lax.axis_size("tgt")
    first_row = lax.axis_index("tgt") * share_rows
    overall = lax.pmax(local_top, "tgt")
    factor = jnp.exp(local_top - overall)
    numerator = numerator * factor[:, None]
    denominator = denominator * factor
    numerator, denominator = lax.psum((numerator, denominator), "tgt")
    numerator = lax.dynamic_slice_in_dim(numerator, first_row, share_rows, 0)
    denominator = lax.dynamic_slice_in_dim(denominator, first_row, share_rows, 0)
    projected = numerator / denominator[:, None]
    return (projected, src_potential, tgt_potential)


def solution(mesh):
    return jax.shard_map(
        shards,
        mesh=mesh,
        in_specs=(
            P(None, "src"),
            P(None, "tgt"),
            P(None, "tgt"),
            P("src"),
            P("tgt"),
            P("src", "tgt"),
            P("src", "tgt"),
        ),
        out_specs=(P(("src", "tgt"), None), P("src"), P("tgt")),
        check_vma=False,
    )
```

profile of v0, /device:TPU:1, one launch (start us, length us, event | category | flops | bytes accessed | tf_op | source)
XLA Modules:
  0.0 761.6 jit_solution(7564907167131679846)
XLA Ops:
  8.1 1.5 multiply_reduce_fusion
  11.3 26.2 %while.70 = (s32[]{:T(128)}, f32[8,256]{1,0:T(8,128)S(1)}, f32[8,256]{1,0:T(8,128)S(1)}, pred[8,8]{1,0:T(8,128)(4,1)S(1)}, s32[8,8]{1,0:T(8,128)S(1)}, /*index=5...) while((s32[]{:T(128)}, f32[8,256]{1,0:T(8,128)S(1)}, ...), condition=%wide.region_5.8_spmd, body=%wide.region_2.7_spmd.sunk | while | flops 72487472 | bytes 5143929 | solution.py:78
  37.5 30.2 %pmax.35 = f32[2048]{0:T(1024)S(1)} all-reduce(f32[2048]{0:T(1024)S(1)} %bitcast.348), channel_id=1, replica_groups=mesh['src'=16,'tgt'=16] {'tgt'}, use_global_device_ids=true, to_apply=%region_6.9 | all-reduce | flops 2048 | bytes 16384 | tf_op jit(solution)/shard_map/pmax | solution.py:20
  67.8 29.3 %psum.42 = f32[2048]{0:T(1024)S(1)} all-reduce(f32[2048]{0:T(1024)S(1)} %exponential_multiply_fusion.3), channel_id=1, replica_groups=mesh['src'=16,'tgt'=16] {'tgt'}, use_global_device_ids=true, to_apply=%region_7.10 | all-reduce | flops 2048 | bytes 16384 | tf_op jit(solution)/shard_map/psum | solution.py:21
  97.1 19.6 %while.71 = (s32[]{:T(128)}, f32[8,8,256]{2,1,0:T(8,128)S(1)}, f32[8,8,256]{2,1,0:T(8,128)S(1)}, pred[8,8]{1,0:T(8,128)(4,1)S(1)}, f32[8,256]{1,0:T(8,128)S(1)},...) while((s32[]{:T(128)}, f32[8,8,256]{2,1,0:T(8,128)S(1)}, ...), condition=%wide.region_11.14_spmd, body=%wide.region_8.13_spmd.sunk | while | flops 72481840 | bytes 5123405 | solution.py:93
  118.2 66.0 %pmax.36 = f32[8192]{0:T(1024)S(1)} all-reduce(f32[8192]{0:T(1024)S(1)} %bitcast.335), channel_id=1, replica_groups=mesh['src'=16,'tgt'=16] {'src'}, use_global_device_ids=true, to_apply=%region_13.16 | all-reduce | flops 8192 | bytes 65536 | tf_op jit(solution)/shard_map/pmax | solution.py:25
  184.3 58.0 %psum.43 = f32[8192]{0:T(1024)S(1)} all-reduce(f32[8192]{0:T(1024)S(1)} %exponential_multiply_fusion.1), channel_id=1, replica_groups=mesh['src'=16,'tgt'=16] {'src'}, use_global_device_ids=true, to_apply=%region_14.18 | all-reduce | flops 8192 | bytes 65536 | tf_op jit(solution)/shard_map/psum | solution.py:26
  242.3 26.1 %while.72 = (s32[]{:T(128)}, f32[8,256]{1,0:T(8,128)S(1)}, f32[8,256]{1,0:T(8,128)S(1)}, pred[8,8]{1,0:T(8,128)(4,1)S(1)}, s32[8,8]{1,0:T(8,128)S(1)}, /*index=5...) while((s32[]{:T(128)}, f32[8,256]{1,0:T(8,128)S(1)}, ...), condition=%wide.region_18.22_spmd, body=%wide.region_15.21_spmd.sunk | while | flops 72487472 | bytes 5111157 | solution.py:78
  268.5 55.3 %pmax.37 = f32[2048]{0:T(1024)S(1)} all-reduce(f32[2048]{0:T(1024)S(1)} %bitcast.350), channel_id=1, replica_groups=mesh['src'=16,'tgt'=16] {'tgt'}, use_global_device_ids=true, to_apply=%region_19.23 | all-reduce | flops 2048 | bytes 16384 | tf_op jit(solution)/shard_map/pmax | solution.py:20
  323.8 27.6 %psum.44 = f32[2048]{0:T(1024)S(1)} all-reduce(f32[2048]{0:T(1024)S(1)} %exponential_multiply_fusion.2), channel_id=1, replica_groups=mesh['src'=16,'tgt'=16] {'tgt'}, use_global_device_ids=true, to_apply=%region_20.24 | all-reduce | flops 2048 | bytes 16384 | tf_op jit(solution)/shard_map/psum | solution.py:21
  352.1 19.6 %while.73 = (s32[]{:T(128)}, f32[8,8,256]{2,1,0:T(8,128)S(1)}, f32[8,8,256]{2,1,0:T(8,128)S(1)}, pred[8,8]{1,0:T(8,128)(4,1)S(1)}, f32[8,256]{1,0:T(8,128)S(1)},...) while((s32[]{:T(128)}, f32[8,8,256]{2,1,0:T(8,128)S(1)}, ...), condition=%wide.region_24.28_spmd, body=%wide.region_21.27_spmd.sunk | while | flops 72481840 | bytes 5123405 | solution.py:93
  373.1 59.6 %pmax.38 = f32[8192]{0:T(1024)S(1)} all-reduce(f32[8192]{0:T(1024)S(1)} %bitcast.337), channel_id=1, replica_groups=mesh['src'=16,'tgt'=16] {'src'}, use_global_device_ids=true, to_apply=%region_26.30 | all-reduce | flops 8192 | bytes 65536 | tf_op jit(solution)/shard_map/pmax | solution.py:25
  432.8 58.6 %psum.45 = f32[8192]{0:T(1024)S(1)} all-reduce(f32[8192]{0:T(1024)S(1)} %exponential_multiply_fusion), channel_id=1, replica_groups=mesh['src'=16,'tgt'=16] {'src'}, use_global_device_ids=true, to_apply=%region_27.31 | all-reduce | flops 8192 | bytes 65536 | tf_op jit(solution)/shard_map/psum | solution.py:26
  492.0 24.2 %while.74 = (s32[]{:T(128)}, f32[8,256]{1,0:T(8,128)S(1)}, pred[8,8]{1,0:T(8,128)(4,1)S(1)}, s32[8,8]{1,0:T(8,128)S(1)}, f32[32,256]{1,0:T(8,128)S(1)}, /*index=...) while((s32[]{:T(128)}, f32[8,256]{1,0:T(8,128)S(1)}, ...), condition=%wide.region_30.34_spmd, body=%wide.region_28.33_spmd.sunk | while | flops 70914864 | bytes 912737 | solution.py:108
  516.2 3.2 copy.51
  519.4 2.9 copy.54
  522.4 55.7 %while.75 = (s32[]{:T(128)}, f32[8,256,128]{2,1,0:T(8,128)}, f32[8,256]{1,0:T(8,128)S(1)}, pred[8,8]{1,0:T(8,128)(4,1)S(1)}, s32[8,8]{1,0:T(8,128)S(1)}, /*index...) while((s32[]{:T(128)}, f32[8,256,128]{2,1,0:T(8,128)}, ...), condition=%wide.region_33.37_spmd, body=%wide.region_31.36_spmd.sunk | while | flops 207492928 | bytes 5770245 | solution.py:124
  525.6 2.2 gather_fusion.16
  532.6 2.2 gather_fusion.16
  539.6 2.2 gather_fusion.16
  545.1 1.4 fusion.128
  546.5 2.2 gather_fusion.16
  552.1 1.4 fusion.128
  553.5 2.2 gather_fusion.16
  560.5 2.2 gather_fusion.16
  567.4 2.2 gather_fusion.16
  574.4 2.2 gather_fusion.16
  578.1 54.6 %pmax.39 = f32[2048]{0:T(1024)S(1)} all-reduce(f32[2048]{0:T(1024)S(1)} %bitcast.346), channel_id=1, replica_groups=mesh['src'=16,'tgt'=16] {'tgt'}, use_global_device_ids=true, to_apply=%region_34.38 | all-reduce | flops 2048 | bytes 16384 | tf_op jit(solution)/shard_map/pmax | solution.py:130
  632.8 2.6 bitcast_multiply_fusion
  635.4 27.6 %psum.47 = f32[2048]{0:T(1024)S(1)} all-reduce(f32[2048]{0:T(1024)S(1)} %get-tuple-element.646), channel_id=1, replica_groups=mesh['src'=16,'tgt'=16] {'tgt'}, use_global_device_ids=true, to_apply=%region_36.40 | all-reduce | flops 2048 | bytes 16384 | tf_op jit(solution)/shard_map/psum | solution.py:134
  663.1 90.1 %all-reduce.2.cloned.1.call-done = f32[2048,128]{1,0:T(8,128)} async-done(((f32[2048,128]{1,0:T(8,128)}), f32[2048,128]{1,0:T(8,128)}) %all-reduce.2.cloned.1.call-update) | async-done | bytes 1048592 | tf_op jit(solution)/shard_map/psum | solution.py:134
  753.2 1.6 dynamic-slice_divide_fusion
  (635 shorter events, 154.4 us)
Async XLA Ops:
  7.2 3.8 copy-start
  7.2 746.0 %all-reduce.2.cloned.1.call-start = ((), (), s32[]{:S(2)}) async-start(), calls=%async_computation | async-start | bytes 2097152 | tf_op jit(solution)/shard_map/psum | solution.py:134
  8.1 3.1 copy-start.6
  8.1 3.2 copy-start.3
  11.3 85.8 %copy-start.5 = (f32[2048]{0:T(1024)S(1)}, f32[2048]{0:T(1024)}, u32[]{:S(2)}) copy-start(f32[2048]{0:T(1024)} %param.28) | copy-start | bytes 24580
  97.1 145.1 %copy-start.2 = (f32[8192]{0:T(1024)S(1)}, f32[8192]{0:T(1024)}, u32[]{:S(2)}) copy-start(f32[8192]{0:T(1024)} %param.29) | copy-start | bytes 98308
  351.5 0.6 copy-start.4
  491.4 0.6 copy-start.1
Sparse Core Ops, SparseCore 0:
  635.5 117.6 all-reduce.1
where the time goes:
time: 762 us
  blocking collectives  467 us (61%)
  local copies, waits for them, and re-layouts  104 us (14%)
  waiting for transfers between devices  90.1 us (12%)
  matrix products  55.5 us (7%)
  other arithmetic  27.1 us (4%)
  between operations  14.5 us (2%)
    pmax x2, blocking collectives, merge_columns(): overall = lax.pmax(block_top, 'src')  126 us
    psum x2, blocking collectives, merge_columns(): return (overall, lax.psum(block_sum * jnp.exp(block_top - overall), 'src'))  117 us
    psum x1, waiting for transfers between devices, shards(): numerator, denominator = lax.psum((numerator, denominator), 'tgt')  90.1 us
    pmax x2, blocking collectives, merge_rows(): overall = lax.pmax(highest, 'tgt')  85.5 us
    psum x2, blocking collectives, merge_rows(): return (overall, lax.psum(totals * jnp.exp(highest - overall), 'tgt'))  56.9 us
    pmax x1, blocking collectives, shards(): overall = lax.pmax(local_top, 'tgt')  54.6 us
    dot_general x48, matrix products, pair_distance(): jnp.einsum('dr,dkc->krc', src_tile, tgt_chosen, preferred_element_type=jn...  45.6 us
    psum x1, blocking collectives, shards(): numerator, denominator = lax.psum((numerator, denominator), 'tgt')  27.6 us
  transfers between devices with their start and end apart: 1, of which 1 were waited for; matrix products, arithmetic and copies ran while one was open for 0% of the time, Pallas kernels for 0%

commit v1 on v0

v1 whole, which is shorter than its diff:
```python
import functools
import math

import jax
import jax.numpy as jnp
from jax import lax
from jax.experimental import pallas as pl
from jax.experimental.pallas import tpu as pltpu
from jax.sharding import PartitionSpec as P

MESH = pl.DeviceIdType.MESH
F32 = jnp.float32
BF16 = jnp.bfloat16

BLOCK = 256
DEPTH = 256
LANES = 128
EPSILON = 0.1
LN2 = math.log(2.0)
SCALE = 1.0 / (EPSILON * LN2)
ABSENT = -1e30
STRIP = 64
TINY = 2.0**-120


def split3(x):
    high = x.astype(BF16).astype(F32)
    rest = x - high
    middle = rest.astype(BF16).astype(F32)
    return high, middle, rest - middle


def iota(shape, dim):
    return lax.broadcasted_iota(jnp.int32, shape, dim)


def dot(a, b):
    return jnp.dot(a, b, preferred_element_type=F32)


def dot_nt(a, b):
    return lax.dot_general(a, b, (((1,), (1,)), ((), ())), preferred_element_type=F32)


def kernel(
    n_src,
    n_tgt,
    kb_ref,
    kc_ref,
    src_ref,
    tgt_ref,
    feat_ref,
    smass_ref,
    tmass_ref,
    proj_ref,
    spot_ref,
    tpot_ref,
    lhs,
    rhs,
    feats,
    plan,
    hot,
    member,
    slots,
    tnorm,
    vpot,
    rows_out,
    rows_in,
    cols_out,
    cols_in,
    back,
    rowtile,
    dens,
    pair_out,
    pair_own,
    pair_in,
    final_in,
    row_send,
    row_recv,
    col_send,
    col_recv,
    back_send,
    back_recv,
    pair_send,
    pair_recv,
    final_send,
    final_recv,
):
    depth = src_ref.shape[0]
    row_blocks = src_ref.shape[1] // BLOCK
    col_blocks = tgt_ref.shape[1] // BLOCK
    slot_count = kb_ref.shape[1]
    all_slots = row_blocks * slot_count
    own_blocks = col_blocks // n_src
    feat = feat_ref.shape[0]
    half = BLOCK // 2

    me_s = lax.axis_index("src")
    me_t = lax.axis_index("tgt")
    chip = me_t // 2
    core = me_t % 2

    barrier = pltpu.get_barrier_semaphore()

    def greet(axis, count, me):
        def body(o, carry):
            pl.semaphore_signal(
                barrier, inc=1, device_id={axis: lax.rem(me + o, count)}, device_id_type=MESH
            )
            return carry

        lax.fori_loop(1, count, body, 0)

    greet("tgt", n_tgt, me_t)
    greet("src", n_src, me_s)

    def row_copy(phase, peer, landing):
        return pltpu.make_async_remote_copy(
            src_ref=rows_out.at[phase],
            dst_ref=rows_in.at[phase, landing],
            send_sem=row_send.at[phase, peer],
            recv_sem=row_recv.at[phase, landing],
            device_id={"tgt": peer},
            device_id_type=MESH,
        )

    def col_copy(phase, peer, landing):
        return pltpu.make_async_remote_copy(
            src_ref=cols_out.at[phase, peer],
            dst_ref=cols_in.at[phase, landing],
            send_sem=col_send.at[phase, peer],
            recv_sem=col_recv.at[phase, landing],
            device_id={"src": peer},
            device_id_type=MESH,
        )

    def back_copy(phase, peer, origin):
        return pltpu.make_async_remote_copy(
            src_ref=back.at[phase, origin],
            dst_ref=back.at[phase, origin],
            send_sem=back_send.at[phase, peer],
            recv_sem=back_recv.at[phase, origin],
            device_id={"src": peer},
            device_id_type=MESH,
        )

    def others(count, me, act):
        def body(o, carry):
            act(lax.rem(me + o, count))
            return carry

        lax.fori_loop(1, count, body, 0)

    def slot_block(r, k):
        return jnp.where(k < kc_ref[r, 0], kb_ref[r, k], col_blocks)

    def v_tile(v):
        high, middle, low = split3(v)
        line = iota((16, BLOCK), 0)
        tile = jnp.where(line < 8, 1.0, 0.0)
        tile = jnp.where(line == 8, high, tile)
        tile = jnp.where(line == 9, middle, tile)
        return jnp.where(line == 10, low, tile).astype(BF16)

    def target_side(s, carry):
        for j in range(own_blocks):
            b = s * own_blocks + j
            y = tgt_ref[:, pl.ds(pl.multiple_of(b * BLOCK, BLOCK), BLOCK)]
            for part in range(3):
                rhs[b, part * depth : (part + 1) * depth, :] = y
            y = y.astype(F32)
            norm = jnp.sum(y * y, axis=0, keepdims=True)
            tnorm[s, j : j + 1, :] = norm
            v = norm * (-SCALE)
            vpot[s, j : j + 1, :] = v
            rhs[b, 3 * depth : 3 * depth + 16, :] = jnp.ones((16, BLOCK), BF16)
            rhs[b, 3 * depth + 16 : 3 * depth + 32, :] = v_tile(v)
            rhs[b, 3 * depth + 32 :, :] = jnp.zeros((DEPTH - 3 * depth - 32, BLOCK), BF16)
        return carry

    lax.fori_loop(0, n_src, target_side, 0)
    rhs[col_blocks, 0 : 3 * depth, :] = jnp.zeros((3 * depth, BLOCK), BF16)
    rhs[col_blocks, 3 * depth : 3 * depth + 16, :] = jnp.ones((16, BLOCK), BF16)
    rhs[col_blocks, 3 * depth + 16 : 3 * depth + 32, :] = v_tile(jnp.full((1, BLOCK), ABSENT, F32))
    rhs[col_blocks, 3 * depth + 32 :, :] = jnp.zeros((DEPTH - 3 * depth - 32, BLOCK), BF16)

    def source_side(r, carry):
        x = src_ref[:, pl.ds(pl.multiple_of(r * BLOCK, BLOCK), BLOCK)].astype(F32)
        line = iota((STRIP, BLOCK), 0)
        strip = jnp.where((line >= 24) & (line < 27), 1.0, 0.0)
        parts = jnp.concatenate([*split3(x * (2.0 * SCALE)), strip], axis=0)
        lhs[r] = parts.T.astype(BF16)
        return carry

    lax.fori_loop(0, row_blocks, source_side, 0)

    def fold(total):
        return total[:, :LANES] + total[:, LANES:]

    def first_rows(r, carry):
        left = lhs[r]
        highest = None
        for k in range(slot_count):
            z = dot(left, rhs[slot_block(r, k)])
            plan[k] = z
            peak = jnp.maximum(z[:, :LANES], z[:, LANES:])
            highest = peak if highest is None else jnp.maximum(highest, peak)
        total = None
        for k in range(slot_count):
            z = plan[k]
            e = jnp.exp2(z[:, :LANES] - highest) + jnp.exp2(z[:, LANES:] - highest)
            total = e if total is None else total + e
        highest, total = highest.T, total.T
        top = jnp.max(highest, axis=0, keepdims=True)
        total = jnp.sum(total * jnp.exp2(highest - top), axis=0, keepdims=True)
        rows_out[0, pl.ds(r, 1), :] = top + jnp.log2(total)
        return carry

    lax.fori_loop(0, row_blocks, first_rows, 0)

    pl.semaphore_wait(barrier, n_src + n_tgt - 2)

    others(n_tgt, me_t, lambda p: row_copy(0, p, me_t).start())
    rows_in[0, me_t] = rows_out[0]

    lane = iota((1, DEPTH), 1)
    lane_slot = lax.rem(lane, all_slots)

    def list_slot(i, kept):
        block = slot_block(i // slot_count, lax.rem(i, slot_count))
        return jnp.where(lane_slot == i, block, kept)

    kept = lax.fori_loop(0, all_slots, list_slot, jnp.full((1, DEPTH), col_blocks, jnp.int32))
    kept = jnp.where(lane < 3 * all_slots, kept, col_blocks)
    wide = (row_blocks * col_blocks, DEPTH)
    line = iota(wide, 0)
    chosen = (kept == lax.rem(line, col_blocks)) & (lane_slot // slot_count == line // col_blocks)
    hot[...] = jnp.where(chosen, 1.0, 0.0).astype(BF16)
    member[...] = jnp.where(kept == iota((col_blocks, DEPTH), 0), 1.0, 0.0).astype(BF16)

    def feature_side(b, carry):
        feats[b, :feat, :] = feat_ref[:, pl.ds(pl.multiple_of(b * BLOCK, BLOCK), BLOCK)]
        feats[b, feat:, :] = jnp.ones((feats.shape[1] - feat, BLOCK), BF16)
        return carry

    lax.fori_loop(0, col_blocks, feature_side, 0)

    def row_lines(ref):
        return jnp.concatenate(
            [ref[:, r * BLOCK : (r + 1) * BLOCK] for r in range(row_blocks)], axis=0
        )

    smass = row_lines(smass_ref)
    own_width = own_blocks * BLOCK
    tmass = tmass_ref[:, pl.ds(pl.multiple_of(me_s * own_width, own_width), own_width)]
    tmass = jnp.concatenate(
        [tmass[:, j * BLOCK : (j + 1) * BLOCK] for j in range(own_blocks)], axis=0
    )

    others(n_tgt, me_t, lambda p: row_copy(0, p, p).wait_recv())
    row_lse = rows_in[0]
    top = jnp.max(row_lse, axis=0)
    u = jnp.log2(smass) - top - jnp.log2(jnp.sum(jnp.exp2(row_lse - top[None]), axis=0))
    strips = jnp.concatenate(
        [
            jnp.zeros((STRIP, BLOCK), F32),
            *split3(u),
            jnp.zeros((LANES - STRIP - 3 * row_blocks, BLOCK), F32),
        ],
        axis=0,
    )
    rowtile[...] = strips.T

    def first_columns(r, carry):
        at = iota((BLOCK, LANES), 1) - STRIP
        spot = (at == r) | (at == r + row_blocks) | (at == r + 2 * row_blocks)
        old = lhs[r, :, LANES:].astype(F32)
        lhs[r, :, LANES:] = jnp.where(spot, rowtile[...], old).astype(BF16)
        left = lhs[r]
        for k in range(slot_count):
            z = dot(left, rhs[slot_block(r, k)])
            highest = jnp.max(z, axis=0, keepdims=True)
            total = jnp.sum(jnp.exp2(z - highest), axis=0, keepdims=True)
            slots[r, k : k + 1, :] = highest + jnp.log2(total)
        return carry

    lax.fori_loop(0, row_blocks, first_columns, 0)

    def slot_parts():
        lines = slots[...].reshape(all_slots, BLOCK)
        parts = [*split3(lines)]
        if 3 * all_slots < DEPTH:
            parts.append(jnp.zeros((DEPTH - 3 * all_slots, BLOCK), F32))
        return jnp.concatenate(parts, axis=0).astype(BF16)

    def send_columns(phase, lines):
        for s in range(n_src):
            cols_out[phase, s] = lines[s * own_blocks : (s + 1) * own_blocks, :]
        others(n_src, me_s, lambda p: col_copy(phase, p, me_s).start())
        cols_in[phase, me_s] = cols_out[phase, me_s]
        others(n_src, me_s, lambda p: col_copy(phase, p, p).wait_recv())

    def send_back(phase, lines):
        back[phase, me_s] = lines
        others(n_src, me_s, lambda p: back_copy(phase, p, me_s).start())

    def wait_back(phase):
        others(n_src, me_s, lambda p: back_copy(phase, p, p).wait_recv())

    present = dot(hot[...], jnp.where(iota((DEPTH, BLOCK), 0) < all_slots, 1.0, 0.0).astype(BF16))
    by_row = jnp.where(present > 0.5, dot(hot[...], slot_parts()), ABSENT)
    by_row = by_row.reshape(row_blocks, col_blocks, BLOCK)
    top = jnp.max(by_row, axis=0)
    send_columns(0, top + jnp.log2(jnp.sum(jnp.exp2(by_row - top[None]), axis=0)))
    col_lse = cols_in[0]
    top = jnp.max(col_lse, axis=0)
    total = jnp.sum(jnp.exp2(col_lse - top[None]), axis=0)
    send_back(0, vpot[me_s] + jnp.log2(tmass) - top - jnp.log2(total))
    wait_back(0)

    def new_potential(s, carry):
        for j in range(own_blocks):
            rhs[s * own_blocks + j, 3 * depth + 16 : 3 * depth + 32, :] = v_tile(
                back[0, s, j : j + 1, :]
            )
        return carry

    lax.fori_loop(0, n_src, new_potential, 0)

    def second_rows(r, carry):
        left = lhs[r]
        total = None
        for k in range(slot_count):
            e = jnp.exp2(dot(left, rhs[slot_block(r, k)]))
            plan[r * slot_count + k] = e
            total = fold(e) if total is None else total + fold(e)
        rows_out[1, pl.ds(r, 1), :] = jnp.sum(total.T, axis=0, keepdims=True)
        return carry

    lax.fori_loop(0, row_blocks, second_rows, 0)
    others(n_tgt, me_t, lambda p: row_copy(1, p, me_t).start())
    rows_in[1, me_t] = rows_out[1]
    snorm = []
    for r in range(row_blocks):
        x = src_ref[:, r * BLOCK : (r + 1) * BLOCK].astype(F32)
        snorm.append(jnp.sum(x * x, axis=0, keepdims=True))
    snorm = jnp.concatenate(snorm, axis=0)
    others(n_tgt, me_t, lambda p: row_copy(1, p, p).wait_recv())
    row_factor = smass / jnp.sum(rows_in[1], axis=0)
    rowtile[...] = jnp.concatenate(
        [row_factor, jnp.zeros((LANES - row_blocks, BLOCK), F32)], axis=0
    ).T

    def second_columns(r, carry):
        at = iota((BLOCK, LANES), 1)
        factor = jnp.sum(jnp.where(at == r, rowtile[...], 0.0), axis=1, keepdims=True)
        for k in range(slot_count):
            e = plan[r * slot_count + k]
            slots[r, k : k + 1, :] = jnp.sum(e * factor, axis=0, keepdims=True)
        return carry

    lax.fori_loop(0, row_blocks, second_columns, 0)
    send_columns(1, dot(member[...], slot_parts()))
    send_back(1, tmass / jnp.sum(cols_in[1], axis=0))
    source_potential = (EPSILON * LN2) * (u + jnp.log2(row_factor)) + snorm
    for r in range(row_blocks):
        spot_ref[:, r * BLOCK : (r + 1) * BLOCK] = source_potential[r : r + 1, :]
    wait_back(1)

    def pair_copy(step):
        return pltpu.make_async_remote_copy(
            src_ref=pair_out.at[step],
            dst_ref=pair_in.at[step],
            send_sem=pair_send.at[step],
            recv_sem=pair_recv.at[step],
            device_id={"tgt": chip * 2 + 1 - core},
            device_id_type=MESH,
        )

    def final_copy(step, r, origin):
        return pltpu.make_async_remote_copy(
            src_ref=pair_own.at[step],
            dst_ref=final_in.at[origin],
            send_sem=final_send.at[step],
            recv_sem=final_recv.at[origin],
            device_id={"tgt": r * 2 + core},
            device_id_type=MESH,
        )

    diagonal = iota((half, LANES), 0) == iota((half, LANES), 1)

    def weigh(step, r):
        highest = None
        for k in range(slot_count):
            b = kb_ref[r, k]
            factor = back[1, b // own_blocks, pl.ds(lax.rem(b, own_blocks), 1), :]
            w = plan[r * slot_count + k] * factor
            plan[r * slot_count + k] = w
            peak = jnp.maximum(w[:, :LANES], w[:, LANES:])
            highest = peak if highest is None else jnp.maximum(highest, peak)
        top = jnp.maximum(jnp.max(highest, axis=1, keepdims=True), TINY)
        scale = 1.0 / top
        total = None
        for k in range(slot_count):
            w = (plan[r * slot_count + k] * scale).astype(BF16)
            part = dot_nt(w, feats[kb_ref[r, k]])
            total = part if total is None else total + part
        total = total * top
        for h in range(2):
            sums = total[h * half : (h + 1) * half]
            den = jnp.sum(jnp.where(diagonal, sums[:, LANES:], 0.0), axis=0, keepdims=True)
            rowtile[h * half : (h + 1) * half, :] = sums[:, :LANES]
            dens[h] = jnp.broadcast_to(den, (8, LANES))

        own = pl.ds(pl.multiple_of(core * half, half), half)
        other = pl.ds(pl.multiple_of((1 - core) * half, half), half)
        pair_out[step, :half, :] = rowtile[other, :]
        pair_out[step, half:, :] = dens[1 - core]
        pair_own[step, :half, :] = rowtile[own, :]
        pair_own[step, half:, :] = dens[core]
        pair_copy(step).start()

    def share(step):
        return lax.rem(chip + 1 + step, row_blocks)

    def forward(step):
        pair_copy(step).wait_recv()
        pair_own[step] = pair_own[step] + pair_in[step]
        final_copy(step, share(step), chip).start()

    weigh(0, share(0))

    def project(step, carry):
        weigh(step, share(step))
        forward(step - 1)
        return carry

    lax.fori_loop(1, row_blocks, project, 0)
    last = row_blocks - 1
    pair_copy(last).wait_recv()
    total = pair_own[last] + pair_in[last]

    def target_out(s, carry):
        for j in range(own_blocks):
            v = back[0, s, j : j + 1, :] + jnp.log2(back[1, s, j : j + 1, :])
            at = pl.ds(pl.multiple_of((s * own_blocks + j) * BLOCK, BLOCK), BLOCK)
            tpot_ref[:, at] = (EPSILON * LN2) * v + tnorm[s, j : j + 1, :]
        return carry

    lax.fori_loop(0, n_src, target_out, 0)

    def collect(step, total):
        origin = share(step)
        final_copy(step, origin, origin).wait_recv()
        return total + final_in[origin]

    total = lax.fori_loop(0, last, collect, total)
    den = jnp.sum(jnp.where(diagonal, total[half : half + 1, :], 0.0), axis=1, keepdims=True)
    proj_ref[...] = total[:half, :] / den

    for phase in range(2):
        others(n_tgt, me_t, lambda p: row_copy(phase, p, me_t).wait_send())
        others(n_src, me_s, lambda p: col_copy(phase, p, me_s).wait_send())
        others(n_src, me_s, lambda p: back_copy(phase, p, me_s).wait_send())

    def drain(step, carry):
        pair_copy(step).wait_send()
        final_copy(step, share(step), chip).wait_send()
        return carry

    lax.fori_loop(0, last, drain, 0)
    pair_copy(last).wait_send()


def shards(n_src, n_tgt, src_emb, tgt_emb, features, src_mass, tgt_mass, kept_blocks, kept_count):
    src_rows, tgt_rows = src_emb.shape[1], tgt_emb.shape[1]
    row_blocks, col_blocks = src_rows // BLOCK, tgt_rows // BLOCK
    slot_count = kept_blocks.shape[1]
    own_blocks = col_blocks // n_src
    share_rows = src_rows // n_tgt
    feat = features.shape[0]
    vmem = pl.BlockSpec(memory_space=pltpu.VMEM)
    smem = pl.BlockSpec(memory_space=pltpu.SMEM)
    message = (row_blocks, share_rows + 8, LANES)
    dma = pltpu.SemaphoreType.DMA
    projected, src_potential, tgt_potential = pl.pallas_call(
        functools.partial(kernel, n_src, n_tgt),
        out_shape=(
            jax.ShapeDtypeStruct((share_rows, feat), F32),
            jax.ShapeDtypeStruct((1, src_rows), F32),
            jax.ShapeDtypeStruct((1, tgt_rows), F32),
        ),
        in_specs=[smem, smem, vmem, vmem, vmem, vmem, vmem],
        out_specs=(vmem, vmem, vmem),
        scratch_shapes=[
            pltpu.VMEM((row_blocks, BLOCK, DEPTH), BF16),
            pltpu.VMEM((col_blocks + 1, DEPTH, BLOCK), BF16),
            pltpu.VMEM((col_blocks, 2 * LANES, BLOCK), BF16),
            pltpu.VMEM((row_blocks * slot_count, BLOCK, BLOCK), F32),
            pltpu.VMEM((row_blocks * col_blocks, DEPTH), BF16),
            pltpu.VMEM((col_blocks, DEPTH), BF16),
            pltpu.VMEM((row_blocks, slot_count, BLOCK), F32),
            pltpu.VMEM((n_src, own_blocks, BLOCK), F32),
            pltpu.VMEM((n_src, own_blocks, BLOCK), F32),
            pltpu.VMEM((2, row_blocks, BLOCK), F32),
            pltpu.VMEM((2, n_tgt, row_blocks, BLOCK), F32),
            pltpu.VMEM((2, n_src, own_blocks, BLOCK), F32),
            pltpu.VMEM((2, n_src, own_blocks, BLOCK), F32),
            pltpu.VMEM((2, n_src, own_blocks, BLOCK), F32),
            pltpu.VMEM((BLOCK, LANES), F32),
            pltpu.VMEM((2, 8, LANES), F32),
            pltpu.VMEM(message, F32),
            pltpu.VMEM(message, F32),
            pltpu.VMEM(message, F32),
            pltpu.VMEM(message, F32),
            dma((2, n_tgt)),
            dma((2, n_tgt)),
            dma((2, n_src)),
            dma((2, n_src)),
            dma((2, n_src)),
            dma((2, n_src)),
            dma((row_blocks,)),
            dma((row_blocks,)),
            dma((row_blocks,)),
            dma((row_blocks,)),
        ],
        compiler_params=pltpu.CompilerParams(
            collective_id=0, has_side_effects=True, vmem_limit_bytes=56 * 1024 * 1024
        ),
        name="transport",
    )(
        kept_blocks,
        kept_count,
        src_emb,
        tgt_emb,
        features,
        src_mass.reshape(1, src_rows),
        tgt_mass.reshape(1, tgt_rows),
    )
    return projected, src_potential.reshape(src_rows), tgt_potential.reshape(tgt_rows)


def solution(mesh):
    return jax.shard_map(
        functools.partial(shards, mesh.shape["src"], mesh.shape["tgt"]),
        mesh=mesh,
        in_specs=(
            P(None, "src"),
            P(None, "tgt"),
            P(None, "tgt"),
            P("src"),
            P("tgt"),
            P("src", "tgt"),
            P("src", "tgt"),
        ),
        out_specs=(P(("src", "tgt"), None), P("src"), P("tgt")),
        check_vma=False,
    )
```

time: 762 us -> 81.2 us (0.11)
  blocking collectives: 467 us -> 0 us
  local copies, waits for them, and re-layouts: 104 us -> 5.46 us
  waiting for transfers between devices: 90.1 us -> 0 us
  Pallas kernels: 0 us -> 74.9 us
  matrix products: 55.5 us -> 0 us
  other arithmetic: 27.1 us -> 0 us
  between operations: 14.5 us -> 0.64 us
    pmax x5 -> x0, blocking collectives: 266 us -> none  [the longest x2 126 us: merge_columns(): overall = lax.pmax(block_top, 'src')]
    psum x5 -> x0, blocking collectives: 201 us -> none  [the longest x2 117 us: merge_columns(): return (overall, lax.psum(block_sum * jnp.exp(block_top - overall), 'src'))]
    gather x138 -> x0, local copies, waits for them, and re-layouts: 90.7 us -> none  [the longest x48 27 us: distances(): jnp.take(target_norm, packet[2], axis=0)]
    psum x1 -> x0, waiting for transfers between devices: 90.1 us -> none  [shards(): numerator, denominator = lax.psum((numerator, denominator), 'tgt')]
    pallas_call x0 -> x1, Pallas kernels: none -> 74.9 us  [shards(): pl.pallas_call(functools.partial(kernel, n_src, n_tgt), out_shape=(jax.Sh...]
    dot_general x58 -> x0, matrix products: 55.5 us -> none  [the longest x48 45.6 us: pair_distance(): jnp.einsum('dr,dkc->krc', src_tile, tgt_chosen, preferred_element_type=jn...]
    reduce_sum x42 -> x0, other arithmetic: 17.2 us -> none  [the longest x16 7.3 us: row_per_block(): jnp.sum(jnp.where(packet[3][:, None, None], jnp.exp(scaled - highest[None...]
  transfers between devices with their start and end apart: 1 -> 0, of which waited for: 1 -> 0; matrix products, arithmetic and copies ran while one was open for 0% -> 0% of each run, Pallas kernels for 0% -> 0%
where the time goes in v1:
time: 81.2 us; the launch traced here: 81 us
  Pallas kernels  74.9 us (92%)
  local copies, waits for them, and re-layouts  5.46 us (7%)
    pallas_call x1, Pallas kernels, shards(): pl.pallas_call(functools.partial(kernel, n_src, n_tgt), out_shape=(jax.Sh...  74.9 us
    unnamed x4, local copies, waits for them, and re-layouts  5.46 us

profile of v1, /device:TPU:1, one launch (start us, length us, event | category | flops | bytes accessed | tf_op | source)
XLA Modules:
  0.0 81.0 jit_solution(3782922470082110438)
XLA Ops:
  0.6 1.3 %copy.10.kc_ref = s32[8,1]{1,0:T(8,128)} copy(s32[8,1]{0,1:T(1,128)} %param.13) | data formatting | bytes 64 | tf_op args[6]
  2.0 74.9 %transport.1 = (f32[128,128]{1,0:T(8,128)}, f32[1,2048]{1,0:T(1,128)}, f32[1,8192]{1,0:T(1,128)}) custom-call(s32[8,8]{1,0:T(8,128)} %kb_ref.1, s32[8,1]{1,0:T(8,128)} %copy.10.kc_ref, bf16[64,2048]{1,0:T(8,128)(2,1)} %src_ref.1, bf16[64,8192]{1,0:T(8,128)(2,1)} %tgt_ref.1, bf16[128,8192]{1,0:T(8,128)(2,1)} %feat_ref.1, f32[1,2048]{1,0:T(1,128)} %bitcast.6, ...), custom_call_target="tpu_custom_call" | custom-call | tf_op jit(solution)/shard_map/transport/pallas_call | solution.py:486
  76.8 1.5 %copy.14 = f32[128,128]{1,0:T(8,128)} copy(f32[128,128]{1,0:T(8,128)} %get-tuple-element.12) | data formatting | bytes 131072
  78.3 1.3 %copy.15 = f32[2048]{0:T(1024)} copy(f32[2048]{0:T(1024)} %bitcast.7) | data formatting | bytes 16384
  79.6 1.4 %copy.16 = f32[8192]{0:T(1024)} copy(f32[8192]{0:T(1024)} %bitcast.5) | data formatting | bytes 65536

commit v2 on v1

v2 whole, which is shorter than its diff:
```python
import functools
import math

import jax
import jax.numpy as jnp
from jax import lax
from jax.experimental import pallas as pl
from jax.experimental.pallas import tpu as pltpu
from jax.sharding import PartitionSpec as P

MESH = pl.DeviceIdType.MESH
F32 = jnp.float32
BF16 = jnp.bfloat16

BLOCK = 256
DEPTH = 256
LANES = 128
EPSILON = 0.1
LN2 = math.log(2.0)
SCALE = 1.0 / (EPSILON * LN2)
ABSENT = -1e30
STRIP = 64
TINY = 2.0**-120
PLANES = 2
ROW_PARTS = 2
LAG = 2


def split3(x):
    high = x.astype(BF16).astype(F32)
    rest = x - high
    middle = rest.astype(BF16).astype(F32)
    return high, middle, rest - middle


def iota(shape, dim):
    return lax.broadcasted_iota(jnp.int32, shape, dim)


def dot(a, b):
    return jnp.dot(a, b, preferred_element_type=F32)


def dot_nt(a, b):
    return lax.dot_general(a, b, (((1,), (1,)), ((), ())), preferred_element_type=F32)


def kernel(
    n_src,
    n_tgt,
    kb_hbm,
    kc_hbm,
    src_hbm,
    tgt_hbm,
    feat_hbm,
    smass_hbm,
    tmass_hbm,
    sums_ref,
    spot_ref,
    tpot_ref,
    kb_ref,
    kc_ref,
    src_ref,
    tgt_ref,
    feat_ref,
    smass_ref,
    tmass_ref,
    lhs,
    rhs,
    feats,
    scores,
    plan,
    hot,
    member,
    slots,
    peaks,
    factors,
    norms,
    u_ref,
    first_out,
    first_in,
    second_out,
    second_in,
    cols_out,
    cols_in,
    back,
    rowtile,
    dens,
    pair_out,
    pair_own,
    pair_in,
    final_in,
    load_sem,
    first_send,
    first_recv,
    second_send,
    second_recv,
    col_send,
    col_recv,
    back_send,
    back_recv,
    pair_send,
    pair_recv,
    final_send,
    final_recv,
):
    depth = src_ref.shape[0]
    row_blocks = src_ref.shape[1] // BLOCK
    col_blocks = tgt_ref.shape[1] // BLOCK
    slot_count = kb_ref.shape[1]
    all_slots = row_blocks * slot_count
    owners = n_src // PLANES
    own_blocks = col_blocks // owners
    feat = feat_ref.shape[0]
    half = BLOCK // 2
    row_parts, part_rows = first_out.shape[0], first_out.shape[1]

    me_s = lax.axis_index("src")
    me_t = lax.axis_index("tgt")
    owner, plane = me_s // PLANES, me_s % PLANES
    chip, core = me_t // 2, me_t % 2

    barrier = pltpu.get_barrier_semaphore()

    def others(count, me, act):
        def body(i, carry):
            act((me + count // 2 + (i + 1) // 2 * (2 * (i % 2) - 1)) % count)
            return carry

        lax.fori_loop(0, count - 1, body, 0)

    def greet(axis, peer):
        pl.semaphore_signal(barrier, inc=1, device_id={axis: peer}, device_id_type=MESH)

    others(n_src, me_s, lambda p: greet("src", p))
    others(n_tgt, me_t, lambda p: greet("tgt", p))

    sources = (src_hbm, tgt_hbm, kb_hbm, kc_hbm, feat_hbm, smass_hbm, tmass_hbm)
    targets = (src_ref, tgt_ref, kb_ref, kc_ref, feat_ref, smass_ref, tmass_ref)
    loads = [
        pltpu.make_async_copy(a, b, load_sem.at[i]) for i, (a, b) in enumerate(zip(sources, targets))
    ]
    for load in loads:
        load.start()

    def first_copy(part, peer, landing):
        return pltpu.make_async_remote_copy(
            src_ref=first_out.at[part],
            dst_ref=first_in.at[part, landing],
            send_sem=first_send.at[part, peer],
            recv_sem=first_recv.at[part, landing],
            device_id={"tgt": peer},
            device_id_type=MESH,
        )

    def second_copy(peer, landing):
        return pltpu.make_async_remote_copy(
            src_ref=second_out,
            dst_ref=second_in.at[landing],
            send_sem=second_send.at[peer],
            recv_sem=second_recv.at[landing],
            device_id={"tgt": peer},
            device_id_type=MESH,
        )

    def col_copy(phase, peer, landing):
        return pltpu.make_async_remote_copy(
            src_ref=cols_out.at[phase, peer // PLANES],
            dst_ref=cols_in.at[phase, landing],
            send_sem=col_send.at[phase, peer],
            recv_sem=col_recv.at[phase, landing],
            device_id={"src": peer},
            device_id_type=MESH,
        )

    def back_copy(phase, peer, origin):
        return pltpu.make_async_remote_copy(
            src_ref=back.at[phase, origin],
            dst_ref=back.at[phase, origin],
            send_sem=back_send.at[phase, peer],
            recv_sem=back_recv.at[phase, origin],
            device_id={"src": peer * PLANES + plane},
            device_id_type=MESH,
        )

    def slot_block(r, k):
        return jnp.where(k < kc_ref[0, r], kb_ref[r, k], col_blocks)

    def v_tile(v):
        high, middle, low = split3(v)
        line = iota((16, BLOCK), 0)
        tile = jnp.where(line < 8, 1.0, 0.0)
        tile = jnp.where(line == 8, high, tile)
        tile = jnp.where(line == 9, middle, tile)
        return jnp.where(line == 10, low, tile).astype(BF16)

    loads[0].wait()

    def source_side(r, carry):
        x = src_ref[:, pl.ds(pl.multiple_of(r * BLOCK, BLOCK), BLOCK)].astype(F32)
        line = iota((STRIP, BLOCK), 0)
        strip = jnp.where((line >= 24) & (line < 27), 1.0, 0.0)
        parts = jnp.concatenate([*split3(x * (2.0 * SCALE)), strip], axis=0)
        lhs[r] = parts.T.astype(BF16)
        return carry

    lax.fori_loop(0, row_blocks, source_side, 0)

    loads[1].wait()

    def target_side(s, carry):
        for j in range(own_blocks):
            b = s * own_blocks + j
            y = tgt_ref[:, pl.ds(pl.multiple_of(b * BLOCK, BLOCK), BLOCK)]
            for part in range(3):
                rhs[b, part * depth : (part + 1) * depth, :] = y
            y = y.astype(F32)
            norm = jnp.sum(y * y, axis=0, keepdims=True)
            norms[s, j : j + 1, :] = norm
            rhs[b, 3 * depth : 3 * depth + 16, :] = jnp.ones((16, BLOCK), BF16)
            rhs[b, 3 * depth + 16 : 3 * depth + 32, :] = v_tile(norm * (-SCALE))
            rhs[b, 3 * depth + 32 :, :] = jnp.zeros((DEPTH - 3 * depth - 32, BLOCK), BF16)
        return carry

    lax.fori_loop(0, owners, target_side, 0)
    rhs[col_blocks, 0 : 3 * depth, :] = jnp.zeros((3 * depth, BLOCK), BF16)
    rhs[col_blocks, 3 * depth : 3 * depth + 16, :] = jnp.ones((16, BLOCK), BF16)
    rhs[col_blocks, 3 * depth + 16 : 3 * depth + 32, :] = v_tile(jnp.full((1, BLOCK), ABSENT, F32))
    rhs[col_blocks, 3 * depth + 32 :, :] = jnp.zeros((DEPTH - 3 * depth - 32, BLOCK), BF16)

    loads[2].wait()
    loads[3].wait()

    def first_rows(r, carry):
        left = lhs[r]
        highest = None
        for k in range(slot_count):
            z = dot(left, rhs[slot_block(r, k)])
            scores[k] = z
            peak = jnp.maximum(z[:, :LANES], z[:, LANES:])
            highest = peak if highest is None else jnp.maximum(highest, peak)
        total = None
        for k in range(slot_count):
            z = scores[k]
            e = jnp.exp2(z[:, :LANES] - highest) + jnp.exp2(z[:, LANES:] - highest)
            total = e if total is None else total + e
        highest, total = highest.T, total.T
        top = jnp.max(highest, axis=0, keepdims=True)
        total = jnp.sum(total * jnp.exp2(highest - top), axis=0, keepdims=True)
        first_out[r // part_rows, pl.ds(r % part_rows, 1), :] = top + jnp.log2(total)
        return carry

    for part in range(row_parts):
        lax.fori_loop(part * part_rows, (part + 1) * part_rows, first_rows, 0)
        if part == 0:
            pl.semaphore_wait(barrier, n_src + n_tgt - 2)
        others(n_tgt, me_t, lambda p: first_copy(part, p, me_t).start())
        first_in[part, me_t] = first_out[part]

    lane = iota((1, DEPTH), 1)
    lane_slot = lane & (all_slots - 1)

    def list_slot(i, kept):
        block = slot_block(i // slot_count, i % slot_count)
        return jnp.where(lane_slot == i, block, kept)

    kept = lax.fori_loop(0, all_slots, list_slot, jnp.full((1, DEPTH), col_blocks, jnp.int32))
    kept = jnp.where(lane < 3 * all_slots, kept, col_blocks)
    member[...] = jnp.where(kept == iota((col_blocks, DEPTH), 0), 1.0, 0.0).astype(BF16)
    for r in range(row_blocks):
        here = (lane_slot >= r * slot_count) & (lane_slot < (r + 1) * slot_count)
        mine = jnp.where(here, kept, col_blocks)
        hot[r * col_blocks : (r + 1) * col_blocks, :] = jnp.where(
            mine == iota((col_blocks, DEPTH), 0), 1.0, 0.0
        ).astype(BF16)
    u_ref[...] = jnp.zeros_like(u_ref)
    loads[5].wait()
    loads[6].wait()

    def first_columns(r, carry):
        at = iota((BLOCK, LANES), 1) - STRIP
        spot = (at == r) | (at == r + row_blocks) | (at == r + 2 * row_blocks)
        old = lhs[r, :, LANES:].astype(F32)
        lhs[r, :, LANES:] = jnp.where(spot, rowtile[...], old).astype(BF16)
        left = lhs[r]
        for k in range(slot_count):
            z = dot(left, rhs[slot_block(r, k)])
            highest = jnp.max(z, axis=0, keepdims=True)
            e = jnp.exp2(z - highest)
            plan[r * slot_count + k] = e
            total = jnp.sum(e, axis=0, keepdims=True)
            peaks[r, k : k + 1, :] = highest
            slots[r, k : k + 1, :] = highest + jnp.log2(total)
        return carry

    for part in range(row_parts):
        rows = slice(part * part_rows, (part + 1) * part_rows)
        others(n_tgt, me_t, lambda p: first_copy(part, p, p).wait_recv())
        row_lse = first_in[part]
        top = jnp.max(row_lse, axis=0)
        total = jnp.sum(jnp.exp2(row_lse - top[None]), axis=0)
        for i in range(part_rows):
            r = part * part_rows + i
            u_ref[r : r + 1, :] = (
                jnp.log2(smass_ref[:, r * BLOCK : (r + 1) * BLOCK])
                - top[i : i + 1, :]
                - jnp.log2(total[i : i + 1, :])
            )
        strips = jnp.concatenate(
            [
                jnp.zeros((STRIP, BLOCK), F32),
                *split3(u_ref[...]),
                jnp.zeros((LANES - STRIP - 3 * row_blocks, BLOCK), F32),
            ],
            axis=0,
        )
        rowtile[...] = strips.T
        lax.fori_loop(part * part_rows, (part + 1) * part_rows, first_columns, 0)

    def slot_parts():
        lines = slots[...].reshape(all_slots, BLOCK)
        parts = [*split3(lines)]
        if 3 * all_slots < DEPTH:
            parts.append(jnp.zeros((DEPTH - 3 * all_slots, BLOCK), F32))
        return jnp.concatenate(parts, axis=0).astype(BF16)

    def send_columns(phase, lines):
        for s in range(owners):
            cols_out[phase, s] = lines[s * own_blocks : (s + 1) * own_blocks, :]
        others(n_src, me_s, lambda p: col_copy(phase, p, me_s).start())
        cols_in[phase, me_s] = cols_out[phase, owner]

    def wait_columns(phase):
        others(n_src, me_s, lambda p: col_copy(phase, p, p).wait_recv())
        return cols_in[phase]

    def send_back(phase, lines):
        back[phase, owner] = lines
        others(owners, owner, lambda p: back_copy(phase, p, owner).start())

    def wait_back(phase):
        others(owners, owner, lambda p: back_copy(phase, p, p).wait_recv())

    present = dot(hot[...], jnp.where(iota((DEPTH, BLOCK), 0) < all_slots, 1.0, 0.0).astype(BF16))
    by_row = jnp.where(present > 0.5, dot(hot[...], slot_parts()), ABSENT)
    by_row = by_row.reshape(row_blocks, col_blocks, BLOCK)
    top = jnp.max(by_row, axis=0)
    send_columns(0, top + jnp.log2(jnp.sum(jnp.exp2(by_row - top[None]), axis=0)))

    own_width = own_blocks * BLOCK
    tmass = tmass_ref[:, pl.ds(pl.multiple_of(owner * own_width, own_width), own_width)]
    tmass = jnp.concatenate(
        [tmass[:, j * BLOCK : (j + 1) * BLOCK] for j in range(own_blocks)], axis=0
    )
    tmass_log = jnp.log2(tmass)
    loads[4].wait()

    def feature_side(b, carry):
        feats[b, :feat, :] = feat_ref[:, pl.ds(pl.multiple_of(b * BLOCK, BLOCK), BLOCK)]
        feats[b, feat:, :] = jnp.ones((feats.shape[1] - feat, BLOCK), BF16)
        return carry

    lax.fori_loop(0, col_blocks, feature_side, 0)

    col_lse = wait_columns(0)
    top = jnp.max(col_lse, axis=0)
    total = jnp.sum(jnp.exp2(col_lse - top[None]), axis=0)
    send_back(0, tmass_log - top - jnp.log2(total))
    snorm = []
    for r in range(row_blocks):
        x = src_ref[:, r * BLOCK : (r + 1) * BLOCK].astype(F32)
        snorm.append(jnp.sum(x * x, axis=0, keepdims=True))
    wait_back(0)

    def back_line(phase, b):
        return back[phase, b // own_blocks, pl.ds(b % own_blocks, 1), :]

    def second_rows(r, carry):
        total = None
        for k in range(slot_count):
            factor = jnp.exp2(peaks[r, k : k + 1, :] + back_line(0, kb_ref[r, k]))
            factors[r, k : k + 1, :] = factor
            e = plan[r * slot_count + k] * factor
            e = e[:, :LANES] + e[:, LANES:]
            total = e if total is None else total + e
        second_out[pl.ds(r, 1), :] = jnp.sum(total.T, axis=0, keepdims=True)
        return carry

    lax.fori_loop(0, row_blocks, second_rows, 0)
    others(n_tgt, me_t, lambda p: second_copy(p, me_t).start())
    second_in[me_t] = second_out[...]
    snorm = jnp.concatenate(snorm, axis=0)
    smass = jnp.concatenate(
        [smass_ref[:, r * BLOCK : (r + 1) * BLOCK] for r in range(row_blocks)], axis=0
    )
    others(n_tgt, me_t, lambda p: second_copy(p, p).wait_recv())
    row_factor = smass / jnp.sum(second_in[...], axis=0)
    rowtile[...] = jnp.concatenate(
        [row_factor, jnp.zeros((LANES - row_blocks, BLOCK), F32)], axis=0
    ).T

    def second_columns(r, carry):
        at = iota((BLOCK, LANES), 1)
        factor = jnp.sum(jnp.where(at == r, rowtile[...], 0.0), axis=1, keepdims=True)
        for k in range(slot_count):
            e = plan[r * slot_count + k]
            slots[r, k : k + 1, :] = factors[r, k : k + 1, :] * jnp.sum(
                e * factor, axis=0, keepdims=True
            )
        return carry

    lax.fori_loop(0, row_blocks, second_columns, 0)
    send_columns(1, dot(member[...], slot_parts()))
    source_potential = (EPSILON * LN2) * (u_ref[...] + jnp.log2(row_factor)) + snorm
    for r in range(row_blocks):
        spot_ref[:, r * BLOCK : (r + 1) * BLOCK] = source_potential[r : r + 1, :]
    send_back(1, tmass / jnp.sum(wait_columns(1), axis=0))
    wait_back(1)

    def pair_copy(step):
        return pltpu.make_async_remote_copy(
            src_ref=pair_out.at[step],
            dst_ref=pair_in.at[step],
            send_sem=pair_send.at[step],
            recv_sem=pair_recv.at[step],
            device_id={"tgt": chip * 2 + 1 - core},
            device_id_type=MESH,
        )

    def final_copy(step, r, origin):
        return pltpu.make_async_remote_copy(
            src_ref=pair_own.at[step],
            dst_ref=final_in.at[origin],
            send_sem=final_send.at[step],
            recv_sem=final_recv.at[origin],
            device_id={"tgt": r * 2 + core},
            device_id_type=MESH,
        )

    diagonal = iota((half, LANES), 0) == iota((half, LANES), 1)

    def weigh(step, r):
        highest = None
        scales = []
        for k in range(slot_count):
            scales.append(factors[r, k : k + 1, :] * back_line(1, kb_ref[r, k]))
            w = plan[r * slot_count + k] * scales[k]
            peak = jnp.maximum(w[:, :LANES], w[:, LANES:])
            highest = peak if highest is None else jnp.maximum(highest, peak)
        top = jnp.maximum(jnp.max(highest, axis=1, keepdims=True), TINY)
        scale = 1.0 / top
        total = None
        for k in range(slot_count):
            w = (plan[r * slot_count + k] * scales[k] * scale).astype(BF16)
            part = dot_nt(w, feats[kb_ref[r, k]])
            total = part if total is None else total + part
        total = total * top
        for h in range(2):
            sums = total[h * half : (h + 1) * half]
            den = jnp.sum(jnp.where(diagonal, sums[:, LANES:], 0.0), axis=0, keepdims=True)
            rowtile[h * half : (h + 1) * half, :] = sums[:, :LANES]
            dens[h] = jnp.broadcast_to(den, (8, LANES))

        own = pl.ds(pl.multiple_of(core * half, half), half)
        other = pl.ds(pl.multiple_of((1 - core) * half, half), half)
        pair_out[step, :half, :] = rowtile[other, :]
        pair_out[step, half:, :] = dens[1 - core]
        pair_copy(step).start()
        pair_own[step, :half, :] = rowtile[own, :]
        pair_own[step, half:, :] = dens[core]

    def share(step):
        return (chip + 1 + step) % row_blocks

    def forward(step):
        pair_copy(step).wait_recv()
        pair_own[step] = pair_own[step] + pair_in[step]
        final_copy(step, share(step), chip).start()

    last = row_blocks - 1
    for step in range(LAG):
        weigh(step, share(step))

    def project(step, carry):
        weigh(step, share(step))
        forward(step - LAG)
        return carry

    lax.fori_loop(LAG, row_blocks, project, 0)
    for step in range(row_blocks - LAG, last):
        forward(step)
    pair_copy(last).wait_recv()
    total = pair_own[last] + pair_in[last]

    def target_out(s, carry):
        for j in range(own_blocks):
            v = back[0, s, j : j + 1, :] + jnp.log2(back[1, s, j : j + 1, :])
            norm = norms[s, j : j + 1, :]
            at = pl.ds(pl.multiple_of((s * own_blocks + j) * BLOCK, BLOCK), BLOCK)
            tpot_ref[:, at] = (EPSILON * LN2) * (v - SCALE * norm) + norm
        return carry

    lax.fori_loop(0, owners, target_out, 0)

    for phase in range(2):
        others(n_src, me_s, lambda p: col_copy(phase, p, me_s).wait_send())
        others(owners, owner, lambda p: back_copy(phase, p, owner).wait_send())
    for part in range(row_parts):
        others(n_tgt, me_t, lambda p: first_copy(part, p, me_t).wait_send())
    others(n_tgt, me_t, lambda p: second_copy(p, me_t).wait_send())

    def collect(step, total):
        origin = share(step)
        final_copy(step, origin, origin).wait_recv()
        return total + final_in[origin]

    sums_ref[...] = lax.fori_loop(0, last, collect, total)

    def drain(step, carry):
        pair_copy(step).wait_send()
        final_copy(step, share(step), chip).wait_send()
        return carry

    lax.fori_loop(0, last, drain, 0)
    pair_copy(last).wait_send()


def finish(sums_ref, spot_in, tpot_in, proj_ref, spot_ref, tpot_ref):
    rows, lanes = proj_ref.shape
    diagonal = iota((rows, lanes), 0) == iota((rows, lanes), 1)
    den = jnp.sum(jnp.where(diagonal, sums_ref[rows : rows + 1, :], 0.0), axis=1, keepdims=True)
    proj_ref[...] = sums_ref[:rows, :] / den
    spot_ref[...] = spot_in[...]
    tpot_ref[...] = tpot_in[...]


def shards(n_src, n_tgt, src_emb, tgt_emb, features, src_mass, tgt_mass, kept_blocks, kept_count):
    src_rows, tgt_rows = src_emb.shape[1], tgt_emb.shape[1]
    row_blocks, col_blocks = src_rows // BLOCK, tgt_rows // BLOCK
    slot_count = kept_blocks.shape[1]
    owners = n_src // PLANES
    own_blocks = col_blocks // owners
    share_rows = src_rows // n_tgt
    feat = features.shape[0]
    part_rows = row_blocks // ROW_PARTS
    vmem = pl.BlockSpec(memory_space=pltpu.VMEM)
    anywhere = pl.BlockSpec(memory_space=pl.ANY)
    message = (row_blocks, share_rows + 8, LANES)
    dma = pltpu.SemaphoreType.DMA
    operands = (
        kept_blocks,
        kept_count.reshape(1, row_blocks),
        src_emb,
        tgt_emb,
        features,
        src_mass.reshape(1, src_rows),
        tgt_mass.reshape(1, tgt_rows),
    )
    landing = [
        (pltpu.SMEM if x.dtype == jnp.int32 else pltpu.VMEM)(x.shape, x.dtype) for x in operands
    ]
    out_lines = (
        jax.ShapeDtypeStruct((1, src_rows), F32),
        jax.ShapeDtypeStruct((1, tgt_rows), F32),
    )
    results = pl.pallas_call(
        functools.partial(kernel, n_src, n_tgt),
        out_shape=(jax.ShapeDtypeStruct((share_rows + 8, feat), F32), *out_lines),
        in_specs=[anywhere] * 7,
        out_specs=(vmem, vmem, vmem),
        scratch_shapes=[
            *landing,
            pltpu.VMEM((row_blocks, BLOCK, DEPTH), BF16),
            pltpu.VMEM((col_blocks + 1, DEPTH, BLOCK), BF16),
            pltpu.VMEM((col_blocks, 2 * LANES, BLOCK), BF16),
            pltpu.VMEM((slot_count, BLOCK, BLOCK), F32),
            pltpu.VMEM((row_blocks * slot_count, BLOCK, BLOCK), F32),
            pltpu.VMEM((row_blocks * col_blocks, DEPTH), BF16),
            pltpu.VMEM((col_blocks, DEPTH), BF16),
            pltpu.VMEM((row_blocks, slot_count, BLOCK), F32),
            pltpu.VMEM((row_blocks, slot_count, BLOCK), F32),
            pltpu.VMEM((row_blocks, slot_count, BLOCK), F32),
            pltpu.VMEM((owners, own_blocks, BLOCK), F32),
            pltpu.VMEM((row_blocks, BLOCK), F32),
            pltpu.VMEM((ROW_PARTS, part_rows, BLOCK), F32),
            pltpu.VMEM((ROW_PARTS, n_tgt, part_rows, BLOCK), F32),
            pltpu.VMEM((row_blocks, BLOCK), F32),
            pltpu.VMEM((n_tgt, row_blocks, BLOCK), F32),
            pltpu.VMEM((2, owners, own_blocks, BLOCK), F32),
            pltpu.VMEM((2, n_src, own_blocks, BLOCK), F32),
            pltpu.VMEM((2, owners, own_blocks, BLOCK), F32),
            pltpu.VMEM((BLOCK, LANES), F32),
            pltpu.VMEM((2, 8, LANES), F32),
            pltpu.VMEM(message, F32),
            pltpu.VMEM(message, F32),
            pltpu.VMEM(message, F32),
            pltpu.VMEM(message, F32),
            dma((7,)),
            dma((ROW_PARTS, n_tgt)),
            dma((ROW_PARTS, n_tgt)),
            dma((n_tgt,)),
            dma((n_tgt,)),
            dma((2, n_src)),
            dma((2, n_src)),
            dma((2, owners)),
            dma((2, owners)),
            dma((row_blocks,)),
            dma((row_blocks,)),
            dma((row_blocks,)),
            dma((row_blocks,)),
        ],
        compiler_params=pltpu.CompilerParams(
            collective_id=0, has_side_effects=True, vmem_limit_bytes=56 * 1024 * 1024
        ),
        name="transport",
    )(*operands)
    projected, src_potential, tgt_potential = pl.pallas_call(
        finish,
        out_shape=(jax.ShapeDtypeStruct((share_rows, feat), F32), *out_lines),
        in_specs=[vmem] * 3,
        out_specs=(vmem,) * 3,
        name="finish",
    )(*results)
    return projected, src_potential.reshape(src_rows), tgt_potential.reshape(tgt_rows)


def solution(mesh):
    return jax.shard_map(
        functools.partial(shards, mesh.shape["src"], mesh.shape["tgt"]),
        mesh=mesh,
        in_specs=(
            P(None, "src"),
            P(None, "tgt"),
            P(None, "tgt"),
            P("src"),
            P("tgt"),
            P("src", "tgt"),
            P("src", "tgt"),
        ),
        out_specs=(P(("src", "tgt"), None), P("src"), P("tgt")),
        check_vma=False,
    )
```

time: 81.2 us -> 70 us (0.86)
  Pallas kernels: 74.9 us -> 68.4 us
  local copies, waits for them, and re-layouts: 5.46 us -> 0 us
    pallas_call x1, Pallas kernels: 74.9 us -> 66.8 us  [shards(): pl.pallas_call(functools.partial(kernel, n_src, n_tgt), out_shape=(jax.Sh...]
    unnamed x4 -> x0, local copies, waits for them, and re-layouts: 5.46 us -> none
    pallas_call x0 -> x1, Pallas kernels: none -> 1.64 us  [shards(): pl.pallas_call(finish, out_shape=(jax.ShapeDtypeStruct((share_rows, feat)...]
where the time goes in v2:
time: 70 us; the launch traced here: 69.1 us
  Pallas kernels  68.4 us (98%)
    pallas_call x1, Pallas kernels, shards(): pl.pallas_call(functools.partial(kernel, n_src, n_tgt), out_shape=(jax.Sh...  66.8 us
    pallas_call x1, Pallas kernels, shards(): pl.pallas_call(finish, out_shape=(jax.ShapeDtypeStruct((share_rows, feat)...  1.64 us

profile of v2, /device:TPU:1, one launch (start us, length us, event | category | flops | bytes accessed | tf_op | source)
XLA Modules:
  0.0 69.1 jit_solution(7802231253817931614)
XLA Ops:
  0.6 66.8 %transport.1 = (f32[136,128]{1,0:T(8,128)}, f32[1,2048]{1,0:T(1,128)}, f32[1,8192]{1,0:T(1,128)}) custom-call(s32[8,8]{1,0:T(8,128)} %kb_hbm.1, s32[1,8]{1,0:T(1,128)} %bitcast.7, bf16[64,2048]{1,0:T(8,128)(2,1)} %src_hbm.1, bf16[64,8192]{1,0:T(8,128)(2,1)} %tgt_hbm.1, bf16[128,8192]{1,0:T(8,128)(2,1)} %feat_hbm.1, f32[1,2048]{1,0:T(1,128)} %bitcast.6, ...), custom_call_target="tpu_custom_call" | custom-call | tf_op jit(solution)/shard_map/transport/pallas_call | solution.py:566
  67.4 1.6 %finish.1 = (f32[128,128]{1,0:T(8,128)}, f32[1,2048]{1,0:T(1,128)}, f32[1,8192]{1,0:T(1,128)}) custom-call(f32[136,128]{1,0:T(8,128)} %get-tuple-element.9.sums_ref, f32[1,2048]{1,0:T(1,128)} %get-tuple-element.10.spot_in, f32[1,8192]{1,0:T(1,128)} %get-tuple-element.11.tpot_in), custom_call_target="tpu_custom_call" | custom-call | tf_op jit(solution)/shard_map/finish/pallas_call | solution.py:617
